TPU v7x, 128 devices: a whole 4x4x4 slice. The times are simulated.
128 devices in a mesh: row: 4 (over z), col: 32 (over y, x, core).
Axes of the slice: x: 4, y: 4, z: 4, core: 2. Of those that a mesh axis runs over, the one named last changes fastest.
Arguments:
- tokens: bfloat16 [1024, 12288], P('col', 'row'), may hold values from -6 to 6
- cotangent: bfloat16 [1024, 12288], P('col', 'row'), may hold values from -4 to 4
- weight_in: bfloat16 [12288, 24576], P('row', 'col'), may hold values from -0.0546875 to 0.0546875
- bias_in: float32 [24576], P('col'), may hold values from -4 to 4
- weight_out: bfloat16 [24576, 12288], P('col', 'row'), may hold values from -0.0390625 to 0.0390625
Outputs:
- grad_tokens: bfloat16 [1024, 12288], P('col', 'row')
- grad_weight_in: bfloat16 [12288, 24576], P('row', 'col')
- grad_bias_in: float32 [24576], P('col')
- grad_weight_out: bfloat16 [24576, 12288], P('col', 'row')
- grad_bias_out: float32 [12288], P('row')
All inputs are finite; a program needn't handle non-finite values.
Results may differ from a plain program's by a relative error of at most 0.007.
Values may be sent and summed in bfloat16 or wider, within the bound.
A program may use at most 128 MiB of HBM per device.

v0:
```python
import jax
import jax.numpy as jnp
from jax import lax
from jax.sharding import PartitionSpec as P

coeff = 0.7978845608


def act_parts(preact, hidden_grad):
    cube = preact * preact * preact
    tangent = jnp.tanh(coeff * (preact + 0.044715 * cube))
    activated = (0.5 * preact * (1.0 + tangent)).astype(jnp.bfloat16)
    slope = 0.5 * (1.0 + tangent) + 0.5 * preact * (1.0 - tangent * tangent) * coeff * (
        1.0 + 0.134145 * preact * preact
    )
    return (activated, (hidden_grad * slope).astype(jnp.bfloat16))


def input_gradient(preact_grad, weight_in):
    return lax.psum_scatter(
        lax.dot_general(
            preact_grad, weight_in, (((1,), (1,)), ((), ())), preferred_element_type=jnp.float32
        ),
        "col",
        scatter_dimension=0,
        tiled=True,
    ).astype(jnp.bfloat16)


def weight_grads(tok_all, cot_all, activated, preact_grad):
    grad_weight_out = lax.dot_general(
        activated, cot_all, (((0,), (0,)), ((), ())), preferred_element_type=jnp.float32
    ).astype(jnp.bfloat16)
    grad_weight_in = lax.dot_general(
        tok_all, preact_grad, (((0,), (0,)), ((), ())), preferred_element_type=jnp.float32
    ).astype(jnp.bfloat16)
    return (grad_weight_in, grad_weight_out)


def per_device(tokens, cotangent, weight_in, bias_in, weight_out):
    tok_all, cot_all = (
        lax.all_gather(tokens, "col", axis=0, tiled=True),
        lax.all_gather(cotangent, "col", axis=0, tiled=True),
    )
    pre_part = jnp.dot(tok_all, weight_in, preferred_element_type=jnp.float32)
    back_part = lax.dot_general(
        cot_all, weight_out, (((1,), (1,)), ((), ())), preferred_element_type=jnp.float32
    )
    pre_whole, back_whole = lax.psum((pre_part, back_part), "row")
    activated, preact_grad = act_parts(pre_whole + bias_in, back_whole)
    grad_weight_in, grad_weight_out = weight_grads(tok_all, cot_all, activated, preact_grad)
    grad_tokens = input_gradient(preact_grad, weight_in)
    grad_bias_out = jnp.sum(cot_all.astype(jnp.float32), axis=0)
    grad_bias_in = jnp.sum(preact_grad.astype(jnp.float32), axis=0)
    return (grad_tokens, grad_weight_in, grad_bias_in, grad_weight_out, grad_bias_out)


def solution(mesh):
    placed = (P("col", "row"), P("col", "row"), P("row", "col"), P("col"), P("col", "row"))
    return jax.shard_map(
        per_device,
        mesh=mesh,
        in_specs=placed,
        out_specs=(P("col", "row"), P("row", "col"), P("col"), P("col", "row"), P("row")),
        check_vma=False,
    )
```

profile of v0, /device:TPU:1, one launch (start us, length us, event | category | flops | bytes accessed | tf_op | source)
XLA Modules:
  0.0 375.3 jit_solution(4903745220964298293)
XLA Ops:
  7.2 0.0 all-gather.3.cloned.1.call-start
  7.2 0.7 all-gather.3.cloned.1.call-update
  7.9 0.0 all-gather.5.cloned.1.call-start
  7.9 0.7 all-gather.5.cloned.1.call-update
  8.6 0.0 all-reduce.3.cloned.1.call-start
  8.7 54.2 %all-gather.3.cloned.1.call-done = bf16[1024,3072]{1,0:T(8,128)(2,1)} async-done(((bf16[32,3072]{1,0:T(8,128)(2,1)}), bf16[1024,3072]{1,0:T(8,128)(2,1)}) %all-gather.3.cloned.1.call-update) | async-done | bytes 6291472 | tf_op jit(solution)/shard_map/all_gather | solution.py:43
  62.9 9.7 %fusion.20 = f32[1024,768]{1,0:T(8,128)} fusion(bf16[1024,3072]{1,0:T(8,128)(2,1)} %all-gather.3.cloned.1.call-done, bf16[768,3072]{1,0:T(8,128)(2,1)} %param.9), kind=kOutput, calls=%fused_computation.26 | convolution fusion | flops 4831838208 | bytes 14155776 | tf_op jit(solution)/shard_map/dot_general | solution.py:46
  72.6 40.6 %all-gather.5.cloned.1.call-done = bf16[1024,3072]{1,0:T(8,128)(2,1)} async-done(((bf16[32,3072]{1,0:T(8,128)(2,1)}), bf16[1024,3072]{1,0:T(8,128)(2,1)}) %all-gather.5.cloned.1.call-update) | async-done | bytes 6291472 | tf_op jit(solution)/shard_map/all_gather | solution.py:42
  113.2 9.6 %fusion.21 = f32[1024,768]{1,0:T(8,128)} fusion(bf16[1024,3072]{1,0:T(8,128)(2,1)} %all-gather.5.cloned.1.call-done, bf16[3072,768]{1,0:T(8,128)(2,1)} %param.7), kind=kOutput, calls=%fused_computation.27 | convolution fusion | flops 4831838208 | bytes 14155776 | tf_op jit(solution)/shard_map/dot_general | solution.py:45
  122.8 0.0 copy-start.1
  122.9 0.0 all-reduce.3.cloned.1.call-update
  122.9 0.2 reduce-scatter.2.cloned.1.call-start
  123.1 125.8 %all-reduce.3.cloned.1.call-done = (f32[1024,768]{1,0:T(8,128)}, f32[1024,768]{1,0:T(8,128)}) async-done(((f32[1024,768]{1,0:T(8,128)}, f32[1024,768]{1,0:T(8,128)}), (f32[1024,768]{1,0:T(8,128)}, f32[1024,768]{1,0:T(8,128)})) %all-reduce.3.cloned.1.call-update) | async-done | bytes 6291472 | tf_op jit(solution)/shard_map/psum | solution.py:49
  248.9 0.0 copy-done.1
  249.0 4.7 %convert_reduce_fusion.1 = (f32[768]{0:T(1024)}, bf16[1024,768]{1,0:T(8,128)(2,1)S(1)}) fusion(f32[1024,768]{1,0:T(8,128)} %get-tuple-element.10, f32[1024,768]{1,0:T(8,128)} %get-tuple-element.11, f32[768]{0:T(1024)S(1)} %copy-done.1), kind=kLoop, calls=%fused_computation.16 | loop fusion | flops 17300736 | bytes 7870464 | tf_op jit(solution)/shard_map/reduce_sum | solution.py:54
  253.7 10.3 %fusion.22 = f32[1024,3072]{1,0:T(8,128)} fusion(bf16[1024,768]{1,0:T(8,128)(2,1)S(1)} %get-tuple-element.13, bf16[3072,768]{1,0:T(8,128)(2,1)} %param.7), kind=kOutput, calls=%fused_computation.28 | convolution fusion | flops 4831838208 | bytes 18874368 | tf_op jit(solution)/shard_map/dot_general | solution.py:21
  264.0 0.0 reduce-scatter.2.cloned.1.call-update
  264.0 4.3 %convert_reduce_fusion = f32[3072]{0:T(1024)} fusion(bf16[1024,3072]{1,0:T(8,128)(2,1)} %all-gather.3.cloned.1.call-done), kind=kLoop, calls=%fused_computation | loop fusion | flops 6288384 | bytes 6303744 | tf_op jit(solution)/shard_map/reduce_sum | solution.py:53
  268.3 9.5 %fusion = bf16[3072,768]{0,1:T(8,128)(2,1)} fusion(bf16[1024,768]{1,0:T(8,128)(2,1)S(1)} %get-tuple-element.13, bf16[1024,3072]{1,0:T(8,128)(2,1)} %all-gather.5.cloned.1.call-done), kind=kOutput, calls=%fused_computation.5 | convolution fusion | flops 4834197504 | bytes 12582912 | tf_op jit(solution)/shard_map/dot_general | solution.py:34
  277.8 7.1 %copy.10 = bf16[3072,768]{1,0:T(8,128)(2,1)} copy(bf16[3072,768]{0,1:T(8,128)(2,1)} %fusion) | data formatting | bytes 9437184
  284.9 0.0 copy-done
  284.9 10.3 %convolution_convert_fusion = bf16[768,3072]{1,0:T(8,128)(2,1)} fusion(bf16[1024,3072]{1,0:T(8,128)(2,1)} %all-gather.3.cloned.1.call-done, f32[1024,768]{1,0:T(8,128)S(1)} %copy-done, f32[768]{0:T(1024)S(1)} %copy-done.1), kind=kOutput, calls=%fused_computation.1 | convolution fusion | flops 4842061824 | bytes 14158848 | tf_op jit(solution)/shard_map/dot_general | solution.py:31
  295.3 71.8 %reduce-scatter.2.cloned.1.call-done = f32[32,3072]{1,0:T(8,128)} async-done(((f32[1024,3072]{1,0:T(8,128)}), f32[32,3072]{1,0:T(8,128)}) %reduce-scatter.2.cloned.1.call-update) | async-done | bytes 393232 | tf_op jit(solution)/shard_map/reduce_scatter | solution.py:20
  367.1 1.7 convert_element_type.25
  (1 shorter events, 0.0 us)
Async XLA Ops:
  7.2 55.7 %all-gather.3.cloned.1.call-start = ((), (), s32[]{:S(2)}) async-start(), calls=%async_computation.1 | async-start | bytes 6488064 | tf_op jit(solution)/shard_map/all_gather | solution.py:43
  7.9 105.3 %all-gather.5.cloned.1.call-start = ((), (), s32[]{:S(2)}) async-start(), calls=%async_computation.2 | async-start | bytes 6488064 | tf_op jit(solution)/shard_map/all_gather | solution.py:42
  8.6 240.3 %all-reduce.3.cloned.1.call-start = ((), (), s32[]{:S(2)}) async-start(), calls=%async_computation.4 | async-start | bytes 12582912 | tf_op jit(solution)/shard_map/psum | solution.py:49
  122.8 126.1 %copy-start.1 = (f32[768]{0:T(1024)S(1)}, f32[768]{0:T(1024)}, u32[]{:S(2)}) copy-start(f32[768]{0:T(1024)} %param.8) | copy-start | bytes 9220
  122.9 244.2 %reduce-scatter.2.cloned.1.call-start = ((), (), s32[]{:S(2)}) async-start(), calls=%async_computation.3 | async-start | bytes 12976128 | tf_op jit(solution)/shard_map/reduce_scatter | solution.py:20
  277.8 7.1 %copy-start = (f32[1024,768]{1,0:T(8,128)S(1)}, f32[1024,768]{1,0:T(8,128)}, u32[]{:S(2)}) copy-start(f32[1024,768]{1,0:T(8,128)} %get-tuple-element.11) | copy-start | bytes 9437188
Sparse Core Ops, SparseCore 0:
  10.3 52.6 all-gather.2
  65.2 47.9 all-gather.4
  123.0 125.9 all-reduce.2
  264.1 102.9 reduce-scatter.1
where the time goes:
time: 376 us; the launch traced here: 375 us
  waiting for transfers between devices  294 us (78%)
  matrix products  49.5 us (13%)
  between operations  13.8 us (4%)
  other arithmetic  10.7 us (3%)
  local copies, waits for them, and re-layouts  7.13 us (2%)
    psum x1, waiting for transfers between devices, per_device(): pre_whole, back_whole = lax.psum((pre_part, back_part), 'row')  126 us
    reduce_scatter x1, waiting for transfers between devices, input_gradient(): lax.psum_scatter(lax.dot_general(preact_grad, weight_in, (((1,), (1,)), (...  71.8 us
    all_gather x1, waiting for transfers between devices, per_device(): lax.all_gather(cotangent, 'col', axis=0, tiled=True)  54.2 us
    all_gather x1, waiting for transfers between devices, per_device(): lax.all_gather(tokens, 'col', axis=0, tiled=True)  40.6 us
    dot_general x1, matrix products, weight_grads(): lax.dot_general(activated, cot_all, (((0,), (0,)), ((), ())), preferred_e...  10.3 us
    dot_general x1, matrix products, input_gradient(): lax.dot_general(preact_grad, weight_in, (((1,), (1,)), ((), ())), preferr...  10.3 us
    dot_general x1, matrix products, per_device(): lax.dot_general(cot_all, weight_out, (((1,), (1,)), ((), ())), preferred_...  9.73 us
    dot_general x1, matrix products, per_device(): pre_part = jnp.dot(tok_all, weight_in, preferred_element_type=jnp.float32)  9.65 us
  transfers between devices with their start and end apart: 4, of which 4 were waited for; matrix products, arithmetic and copies ran while one was open for 11% of the time, Pallas kernels for 0%

commit v1 on v0

v1 whole, which is shorter than its diff:
```python
import jax
import jax.numpy as jnp
from jax import lax
from jax.experimental import pallas as pl
from jax.experimental.pallas import tpu as pltpu
from jax.sharding import PartitionSpec as P

MESH = pl.DeviceIdType.MESH
coeff = 0.7978845608
N_COPIES = 112
D1 = (0, 1, 3, 2)
CHUNKS = (
    tuple((d, 0) for d in D1),
    ((0, 1), (1, 1), (0, 3), (1, 3)),
    ((3, 1), (2, 1), (3, 3), (2, 3)),
    tuple((d, 2) for d in D1),
)
ROW = {b: c * 256 + i * 32 for c, blocks in enumerate(CHUNKS) for i, b in enumerate(blocks)}


def act_parts(preact, hidden_grad):
    cube = preact * preact * preact
    tangent = jnp.tanh(coeff * (preact + 0.044715 * cube))
    activated = (0.5 * preact * (1.0 + tangent)).astype(jnp.bfloat16)
    slope = 0.5 * (1.0 + tangent) + 0.5 * preact * (1.0 - tangent * tangent) * coeff * (
        1.0 + 0.134145 * preact * preact
    )
    return (activated, (hidden_grad * slope).astype(jnp.bfloat16))


def dot(a, b, ca, cb):
    return lax.dot_general(a, b, (((ca,), (cb,)), ((), ())), preferred_element_type=jnp.float32)


def kernel(
    tok_hbm, cot_hbm, win_hbm, bias_ref, wout_hbm,
    gtok_ref, gwin_hbm, gbin_ref, gwout_hbm, gbout_ref,
    tc, wi, wo, pb, zr, ag, gt, ex, rr, q2, r2, fin, lsem, ssem, rsem,
):
    z = lax.axis_index("row")
    col = lax.axis_index("col")
    y, x, k = col // 8, (col // 2) % 4, col % 2

    def dev(d1=0, d2=0, dz=0, dk=0):
        dx, dy = d1 * (1 - k) + d2 * k, d1 * k + d2 * (1 - k)
        return ((z + dz) % 4, ((y + dy) % 4) * 8 + ((x + dx) % 4) * 2 + (k + dk) % 2)

    used = [0]
    sent = []

    def describe(i, src, dst, device):
        return pltpu.make_async_remote_copy(
            src_ref=src, dst_ref=dst, send_sem=ssem.at[i], recv_sem=rsem.at[i], device_id=device, device_id_type=MESH
        )

    def send(src, dst, device):
        i = used[0]
        used[0] += 1
        cp = describe(i, src, dst, device)
        cp.start()
        sent.append(cp)
        return cp, i

    loads = [
        pltpu.make_async_copy(tok_hbm, tc.at[0, pl.ds(0, 32)], lsem.at[0]),
        pltpu.make_async_copy(cot_hbm, tc.at[1, pl.ds(0, 32)], lsem.at[1]),
        pltpu.make_async_copy(win_hbm, wi, lsem.at[2]),
        pltpu.make_async_copy(wout_hbm, wo, lsem.at[3]),
    ]
    for cp in loads:
        cp.start()

    barrier = pltpu.get_barrier_semaphore()
    greeted = [dev(dk=1)]
    for o in (1, 2, 3):
        greeted += [dev(d1=o), dev(d2=o), dev(dz=o)]
    for device in greeted:
        pl.semaphore_signal(barrier, inc=1, device_id=device, device_id_type=MESH)
    pl.semaphore_wait(barrier, len(greeted))
    loads[0].wait()
    loads[1].wait()

    def block(row):
        return tc.at[:, pl.ds(row, 32)]

    p1, p2, sib = {}, {}, {}

    def share(b):
        sib[b] = send(block(ROW[b]), block(ROW[b] + 128), dev(dk=1))[0]

    for o in (1, 3, 2):
        p1[(-o) % 4] = send(block(0), block(ROW[(-o) % 4, 0]), dev(d1=o))[0]
    share((0, 0))

    def spread(d1):
        for o in (1, 3):
            d2 = (-o) % 4
            p2[d1, d2] = send(block(ROW[d1, 0]), block(ROW[d1, d2]), dev(d2=o))[0]

    def arrive(d1, d2):
        p2[d1, d2].wait_recv()
        if (d2 == 1 and d1 in (0, 3)) or (d2 == 3 and d1 in (1, 2)):
            o = (d2 + 2) % 4
            p2[d1, 2] = send(block(ROW[d1, d2]), block(ROW[d1, 2]), dev(d2=o))[0]
        share((d1, d2))

    zs, agd, fwd2 = {}, {}, {}

    def forward(c):
        for b in CHUNKS[c]:
            sib[b].wait_recv()
        rows = pl.ds(c * 256, 256)
        pb[c, :, 0] = dot(tc[0, rows, :], wi[...], 1, 0).astype(jnp.bfloat16).reshape(4, 64, 768)
        pb[c, :, 1] = dot(tc[1, rows, :], wo[...], 1, 1).astype(jnp.bfloat16).reshape(4, 64, 768)
        for o in (1, 3, 2):
            s = (-o) % 4
            zs[c, s] = send(pb.at[c, (z + o) % 4], zr.at[c, s - 1], dev(dz=o))[0]
        part = jnp.sum(tc[1, rows, :].astype(jnp.float32), axis=0, keepdims=True)
        gbout_ref[...] = part if c == 0 else gbout_ref[...] + part

    def agrows(c, zz, start=0, n=64):
        return ag.at[:, pl.ds(pl.multiple_of(c * 256 + zz * 64 + start, 32), n)]

    def activate(c):
        for s in (1, 3, 2):
            zs[c, s].wait_recv()
        u = bias_ref[...] + pb[c, z, 0].astype(jnp.float32)
        h = pb[c, z, 1].astype(jnp.float32)
        for s in range(3):
            u += zr[c, s, 0].astype(jnp.float32)
            h += zr[c, s, 1].astype(jnp.float32)
        activated, preact_grad = act_parts(u, h)
        mine = pl.ds(pl.multiple_of(c * 256 + z * 64, 64), 64)
        ag[0, mine, :] = activated
        ag[1, mine, :] = preact_grad
        for o in (1, 3):
            agd[c, (-o) % 4] = send(agrows(c, z), agrows(c, z), dev(dz=o))[1]

    def relay(c):
        for s, start in ((1, 0), (3, 32)):
            zz = (z + s) % 4
            describe(agd[c, s], agrows(c, zz), agrows(c, zz), dev(dz=s)).wait_recv()
            fwd2[c, s] = send(agrows(c, zz, start, 32), agrows(c, zz, start, 32), dev(dz=(s + 2) % 4))[1]

    def gathered(c):
        zz = (z + 2) % 4
        for s, start in ((1, 0), (3, 32)):
            half = agrows(c, zz, start, 32)
            describe(fwd2[c, s], half, half, dev(dz=2)).wait_recv()

    exd, rrd = {}, []

    def token_grad(c):
        gathered(c)
        pg = ag[1, pl.ds(c * 256, 256), :]

        @pl.loop(0, 4)
        def _(n):
            cols = pl.ds(pl.multiple_of(n * 768, 768), 768)
            gt[pl.ds(c * 256, 256), cols] = dot(pg, wi[cols, :], 1, 1).astype(jnp.bfloat16)

        exd[c] = send(gt.at[pl.ds(c * 256 + 128, 128)], ex.at[c], dev(dk=1))[0]
        part = jnp.sum(pg.astype(jnp.float32), axis=0, keepdims=True)
        gbin_ref[...] = part if c == 0 else gbin_ref[...] + part

    def combine(c):
        exd[c].wait_recv()
        own = pl.ds(c * 256, 128)
        gt[own, :] = (gt[own, :].astype(jnp.float32) + ex[c].astype(jnp.float32)).astype(jnp.bfloat16)
        if c == 3:
            rrd.append(send(gt.at[own], rr.at[1], dev(d2=2))[0])
        elif c > 0:
            for i, d2 in enumerate((1, 3)):
                src = gt.at[pl.ds(c * 256 + i * 64, 64)]
                rrd.append(send(src, rr.at[(-d2) % 4 - 1, pl.ds((c - 1) * 64, 64)], dev(d2=d2))[0])

    spread(0)
    p1[1].wait_recv()
    share((1, 0))
    spread(1)
    p1[3].wait_recv()
    share((3, 0))
    p1[2].wait_recv()
    share((2, 0))
    spread(3)
    spread(2)
    loads[2].wait()
    loads[3].wait()
    forward(0)
    for b in CHUNKS[1]:
        arrive(*b)
    forward(1)
    activate(0)
    for b in CHUNKS[2]:
        arrive(*b)
    forward(2)
    activate(1)
    relay(0)
    for d1 in D1:
        p2[d1, 2].wait_recv()
        share((d1, 2))
    forward(3)
    activate(2)
    relay(1)
    token_grad(0)
    activate(3)
    relay(2)
    token_grad(1)
    combine(0)
    combine(1)
    relay(3)
    token_grad(2)
    combine(2)
    token_grad(3)
    combine(3)

    @pl.loop(0, 12)
    def _(n):
        cols = pl.ds(pl.multiple_of(n * 256, 256), 256)
        wo[:, cols] = dot(ag[0], tc[1, :, cols], 0, 0).astype(jnp.bfloat16)

    out_wo = pltpu.make_async_copy(wo, gwout_hbm, lsem.at[0])
    out_wo.start()

    for cp in rrd:
        cp.wait_recv()
    r2d = []
    for i, d1 in enumerate(D1):
        rows = pl.ds(i * 32, 32)
        total = gt[rows, :].astype(jnp.float32)
        for s in range(3):
            total += rr[s, rows, :].astype(jnp.float32)
        if d1 == 0:
            fin[...] = total
        else:
            q2[d1 - 1] = total.astype(jnp.bfloat16)
            r2d.append(send(q2.at[d1 - 1], r2.at[(-d1) % 4 - 1], dev(d1=d1))[0])

    @pl.loop(0, 4)
    def _(m):
        cols = pl.ds(pl.multiple_of(m * 768, 768), 768)
        wi[cols, :] = dot(tc[0, :, cols], ag[1], 0, 0).astype(jnp.bfloat16)

    out_wi = pltpu.make_async_copy(wi, gwin_hbm, lsem.at[1])
    out_wi.start()
    for cp in r2d:
        cp.wait_recv()
    total = fin[...]
    for s in range(3):
        total += r2[s].astype(jnp.float32)
    gtok_ref[...] = total.astype(jnp.bfloat16)
    for cp in sent:
        cp.wait_send()
    out_wo.wait()
    out_wi.wait()


def per_device(tokens, cotangent, weight_in, bias_in, weight_out):
    vmem, hbm = pl.BlockSpec(memory_space=pltpu.VMEM), pl.BlockSpec(memory_space=pl.ANY)
    bf16, f32 = jnp.bfloat16, jnp.float32
    grad_tokens, grad_weight_in, grad_bias_in, grad_weight_out, grad_bias_out = pl.pallas_call(
        kernel,
        out_shape=(
            jax.ShapeDtypeStruct((32, 3072), bf16),
            jax.ShapeDtypeStruct((3072, 768), bf16),
            jax.ShapeDtypeStruct((1, 768), f32),
            jax.ShapeDtypeStruct((768, 3072), bf16),
            jax.ShapeDtypeStruct((1, 3072), f32),
        ),
        in_specs=[hbm, hbm, hbm, vmem, hbm],
        out_specs=(vmem, hbm, vmem, hbm, vmem),
        scratch_shapes=[
            pltpu.VMEM((2, 1024, 3072), bf16),
            pltpu.VMEM((3072, 768), bf16),
            pltpu.VMEM((768, 3072), bf16),
            pltpu.VMEM((4, 4, 2, 64, 768), bf16),
            pltpu.VMEM((4, 3, 2, 64, 768), bf16),
            pltpu.VMEM((2, 1024, 768), bf16),
            pltpu.VMEM((1024, 3072), bf16),
            pltpu.VMEM((4, 128, 3072), bf16),
            pltpu.VMEM((3, 128, 3072), bf16),
            pltpu.VMEM((3, 32, 3072), bf16),
            pltpu.VMEM((3, 32, 3072), bf16),
            pltpu.VMEM((32, 3072), f32),
            pltpu.SemaphoreType.DMA((4,)),
            pltpu.SemaphoreType.DMA((N_COPIES,)),
            pltpu.SemaphoreType.DMA((N_COPIES,)),
        ],
        compiler_params=pltpu.CompilerParams(
            collective_id=0, has_side_effects=True, vmem_limit_bytes=60 * 2**20
        ),
        cost_estimate=pl.CostEstimate(flops=24_200_000_000, bytes_accessed=20_000_000, transcendentals=800_000),
    )(tokens, cotangent, weight_in, bias_in.reshape(1, 768), weight_out)
    return (
        grad_tokens,
        grad_weight_in,
        grad_bias_in.reshape(768),
        grad_weight_out,
        grad_bias_out.reshape(3072),
    )


def solution(mesh):
    placed = (P("col", "row"), P("col", "row"), P("row", "col"), P("col"), P("col", "row"))
    return jax.shard_map(
        per_device,
        mesh=mesh,
        in_specs=placed,
        out_specs=(P("col", "row"), P("row", "col"), P("col"), P("col", "row"), P("row")),
        check_vma=False,
    )
```

time: 376 us -> 133 us (0.35)
  waiting for transfers between devices: 294 us -> 0 us
  Pallas kernels: 0 us -> 120 us
  matrix products: 49.5 us -> 0 us
  between operations: 13.8 us -> 0.65 us
  other arithmetic: 10.7 us -> 1.29 us
    psum x1 -> x0, waiting for transfers between devices: 126 us -> none  [per_device(): pre_whole, back_whole = lax.psum((pre_part, back_part), 'row')]
    pallas_call x0 -> x1, Pallas kernels: none -> 120 us  [per_device(): pl.pallas_call(kernel, out_shape=(jax.ShapeDtypeStruct((32, 3072), bf16),...]
    all_gather x2 -> x0, waiting for transfers between devices: 94.8 us -> none  [the longest x1 54.2 us: per_device(): lax.all_gather(cotangent, 'col', axis=0, tiled=True)]
    reduce_scatter x1 -> x0, waiting for transfers between devices: 71.8 us -> none  [input_gradient(): lax.psum_scatter(lax.dot_general(preact_grad, weight_in, (((1,), (1,)), (...]
    dot_general x5 -> x0, matrix products: 49.5 us -> none  [the longest x1 10.3 us: weight_grads(): lax.dot_general(activated, cot_all, (((0,), (0,)), ((), ())), preferred_e...]
    reduce_sum x2 -> x0, other arithmetic: 9.02 us -> none  [the longest x1 4.73 us: per_device(): grad_bias_in = jnp.sum(preact_grad.astype(jnp.float32), axis=0)]
    unnamed x5 -> x10, local copies, waits for them, and re-layouts: 7.13 us -> 9.45 us
  transfers between devices with their start and end apart: 4 -> 0, of which waited for: 4 -> 0; matrix products, arithmetic and copies ran while one was open for 11% -> 0% of each run, Pallas kernels for 0% -> 0%
where the time goes in v1:
time: 133 us
  Pallas kernels  120 us (90%)
  local copies, waits for them, and re-layouts  10.7 us (8%)
    pallas_call x1, Pallas kernels, per_device(): pl.pallas_call(kernel, out_shape=(jax.ShapeDtypeStruct((32, 3072), bf16),...  120 us
    unnamed x10, local copies, waits for them, and re-layouts  9.45 us

profile of v1, /device:TPU:1, one launch (start us, length us, event | category | flops | bytes accessed | tf_op | source)
XLA Modules:
  0.0 132.8 jit_solution(17959315337527683317)
XLA Ops:
  0.6 1.3 reshape.19.bias_ref
  1.9 120.1 %shard_map.92 = (bf16[32,3072]{1,0:T(8,128)(2,1)}, bf16[3072,768]{1,0:T(8,128)(2,1)}, f32[1,768]{1,0:T(1,128)}, bf16[768,3072]{1,0:T(8,128)(2,1)}, f32[1,3072]{1,0:T(1,128)}) custom-call(bf16[32,3072]{1,0:T(8,128)(2,1)} %tok_hbm.1, bf16[32,3072]{1,0:T(8,128)(2,1)} %cot_hbm.1, bf16[3072,768]{1,0:T(8,128)(2,1)} %win_hbm.1, f32[1,768]{1,0:T(1,128)} %reshape.19.bias_ref, ...), custom_call_target="tpu_custom_call" | custom-call | flops 24199999488 | bytes 20000000 | tf_op jit(solution)/shard_map/pallas_call | solution.py:261
  122.0 1.3 reduce
  123.3 0.0 slice-start
  123.3 1.8 %copy.14 = bf16[32,3072]{1,0:T(8,128)(2,1)} copy(bf16[32,3072]{1,0:T(8,128)(2,1)} %get-tuple-element.20) | data formatting | bytes 393216
  125.1 0.0 slice-start.1
  125.1 4.9 %copy.15 = bf16[3072,768]{1,0:T(8,128)(2,1)} copy(bf16[3072,768]{1,0:T(8,128)(2,1)} %get-tuple-element.21) | data formatting | bytes 9437184
  130.0 0.0 slice-done
  130.0 0.0 slice-done.1
  130.0 0.0 copy-start
  130.0 2.2 %copy.16 = bf16[768,3072]{1,0:T(8,128)(2,1)} copy(bf16[768,3072]{1,0:T(8,128)(2,1)S(1)} %bitcast.2) | data formatting | bytes 9437184
  132.2 0.0 copy-done
  132.2 0.6 copy.17
  (1 shorter events, 0.0 us)
Async XLA Ops:
  123.3 6.7 %slice-start = ((s8[4718592]{0:T(1024)(128)(4,1)}), s8[4194304]{0:T(1024)(128)(4,1)S(1)}, s32[]{:S(2)}) async-start(s8[4718592]{0:T(1024)(128)(4,1)} %bitcast.1), calls=%async_computation | async-start | bytes 8388608
  125.1 4.9 %slice-start.1 = ((s8[4718592]{0:T(1024)(128)(4,1)}), s8[524288]{0:T(1024)(128)(4,1)S(1)}, s32[]{:S(2)}) async-start(s8[4718592]{0:T(1024)(128)(4,1)} %bitcast.1), calls=%async_computation.1 | async-start | bytes 1048576
  130.0 2.2 %copy-start = (f32[1,3072]{1,0:T(1,128)S(1)}, f32[1,3072]{1,0:T(1,128)}, u32[]{:S(2)}) copy-start(f32[1,3072]{1,0:T(1,128)} %get-tuple-element.14) | copy-start | bytes 36868

commit v2 on v1

v2 whole, which is shorter than its diff:
```python
import jax
import jax.numpy as jnp
from jax import lax
from jax.experimental import pallas as pl
from jax.experimental.pallas import tpu as pltpu
from jax.sharding import PartitionSpec as P

MESH = pl.DeviceIdType.MESH
coeff = 0.7978845608
N_COPIES = 112
D1 = (0, 1, 3, 2)
CHUNKS = (
    tuple((d, 0) for d in D1),
    ((0, 1), (1, 1), (0, 3), (1, 3)),
    ((3, 1), (2, 1), (3, 3), (2, 3)),
    tuple((d, 2) for d in D1),
)
ROW = {b: c * 256 + i * 32 for c, blocks in enumerate(CHUNKS) for i, b in enumerate(blocks)}


def act_parts(preact, hidden_grad):
    cube = preact * preact * preact
    tangent = jnp.tanh(coeff * (preact + 0.044715 * cube))
    activated = (0.5 * preact * (1.0 + tangent)).astype(jnp.bfloat16)
    slope = 0.5 * (1.0 + tangent) + 0.5 * preact * (1.0 - tangent * tangent) * coeff * (
        1.0 + 0.134145 * preact * preact
    )
    return (activated, (hidden_grad * slope).astype(jnp.bfloat16))


def dot(a, b, ca, cb):
    return lax.dot_general(a, b, (((ca,), (cb,)), ((), ())), preferred_element_type=jnp.float32)


def kernel(
    tok_hbm, cot_hbm, win_hbm, bias_hbm, wout_hbm,
    gtok_ref, wi, gbin_ref, wo, gbout_ref,
    bias, tc, pb, za, zr, ag, gt, ex, rr, q2, r2, fin, lsem, ssem, rsem,
):
    z = lax.axis_index("row")
    col = lax.axis_index("col")
    y, x, k = col // 8, (col // 2) % 4, col % 2

    def dev(d1=0, d2=0, dz=0, dk=0):
        dx, dy = d1 * (1 - k) + d2 * k, d1 * k + d2 * (1 - k)
        return ((z + dz) % 4, ((y + dy) % 4) * 8 + ((x + dx) % 4) * 2 + (k + dk) % 2)

    used = [0]
    sent = []

    def describe(i, src, dst, device):
        return pltpu.make_async_remote_copy(
            src_ref=src, dst_ref=dst, send_sem=ssem.at[i], recv_sem=rsem.at[i], device_id=device, device_id_type=MESH
        )

    def send(src, dst, device):
        i = used[0]
        used[0] += 1
        cp = describe(i, src, dst, device)
        cp.start()
        sent.append(cp)
        return cp, i

    loads = [
        pltpu.make_async_copy(tok_hbm, tc.at[0, pl.ds(0, 32)], lsem.at[0]),
        pltpu.make_async_copy(cot_hbm, tc.at[1, pl.ds(0, 32)], lsem.at[1]),
        pltpu.make_async_copy(win_hbm, wi, lsem.at[2]),
        pltpu.make_async_copy(wout_hbm, wo, lsem.at[3]),
        pltpu.make_async_copy(bias_hbm, bias.at[0], lsem.at[4]),
    ]
    for cp in loads:
        cp.start()

    barrier = pltpu.get_barrier_semaphore()
    greeted = [dev(dk=1)]
    for o in (1, 2, 3):
        greeted += [dev(d1=o), dev(d2=o), dev(dz=o)]
    for device in greeted:
        pl.semaphore_signal(barrier, inc=1, device_id=device, device_id_type=MESH)
    pl.semaphore_wait(barrier, len(greeted))

    def block(row):
        return tc.at[:, pl.ds(row, 32)]

    p1, p2, sib = {}, {}, {}

    def share(b):
        sib[b] = send(block(ROW[b]), block(ROW[b] + 128), dev(dk=1))[0]

    for o in (1, 3, 2):
        rows = pl.ds(ROW[(-o) % 4, 0], 32)
        p1[(-o) % 4] = [send(own, tc.at[i, rows], dev(d1=o))[0] for i, own in enumerate((tok_hbm, cot_hbm))]
    loads[0].wait()
    loads[1].wait()
    share((0, 0))

    def first(d1):
        for cp in p1[d1]:
            cp.wait_recv()
        share((d1, 0))

    def spread(d1):
        for o in (1, 3):
            d2 = (-o) % 4
            p2[d1, d2] = send(block(ROW[d1, 0]), block(ROW[d1, d2]), dev(d2=o))[0]

    def arrive(d1, d2):
        p2[d1, d2].wait_recv()
        if (d2 == 1 and d1 in (0, 3)) or (d2 == 3 and d1 in (1, 2)):
            o = (d2 + 2) % 4
            p2[d1, 2] = send(block(ROW[d1, d2]), block(ROW[d1, 2]), dev(d2=o))[0]
        share((d1, d2))

    zs, agd, fwd2 = {}, {}, {}
    low, high = pl.ds(0, 32), pl.ds(32, 32)

    def part(c, zz, half):
        return pb.at[c, zz % 4, :, half]

    def forward(c):
        for b in CHUNKS[c]:
            sib[b].wait_recv()
        rows = pl.ds(c * 256, 256)
        pb[c, :, 0] = dot(tc[0, rows, :], wi[...], 1, 0).astype(jnp.bfloat16).reshape(4, 64, 768)
        pb[c, :, 1] = dot(tc[1, rows, :], wo[...], 1, 1).astype(jnp.bfloat16).reshape(4, 64, 768)
        for i, (o, near, far) in enumerate(((1, high, low), (3, low, high))):
            zs[c, i, "far"] = send(part(c, z + 2, far), za.at[c, i], dev(dz=o))[0]
            zs[c, i, "near"] = send(part(c, z + o, near), zr.at[c, i, :, near], dev(dz=o))[0]
        total = jnp.sum(tc[1, rows, :].astype(jnp.float32), axis=0, keepdims=True)
        gbout_ref[...] = total if c == 0 else gbout_ref[...] + total

    def pass_on(c):
        for i, (o, far) in enumerate(((1, low), (3, high))):
            zs[c, i, "far"].wait_recv()
            there = (z + o) % 4
            both = pb[c, there, :, far].astype(jnp.float32) + za[c, i].astype(jnp.float32)
            pb[c, there, :, far] = both.astype(jnp.bfloat16)
            zs[c, i, "sum"] = send(part(c, z + o, far), zr.at[c, i, :, far], dev(dz=o))[0]

    def agrows(c, zz, start=0, n=64):
        return ag.at[:, pl.ds(pl.multiple_of(c * 256 + zz * 64 + start, 32), n)]

    def activate(c):
        for i in range(2):
            zs[c, i, "near"].wait_recv()
            zs[c, i, "sum"].wait_recv()
        u = bias[...] + pb[c, z, 0].astype(jnp.float32)
        h = pb[c, z, 1].astype(jnp.float32)
        for i in range(2):
            u += zr[c, i, 0].astype(jnp.float32)
            h += zr[c, i, 1].astype(jnp.float32)
        activated, preact_grad = act_parts(u, h)
        mine = pl.ds(pl.multiple_of(c * 256 + z * 64, 64), 64)
        ag[0, mine, :] = activated
        ag[1, mine, :] = preact_grad
        for o in (1, 3):
            agd[c, (-o) % 4] = send(agrows(c, z), agrows(c, z), dev(dz=o))[1]

    def relay(c):
        for s, start in ((1, 0), (3, 32)):
            zz = (z + s) % 4
            describe(agd[c, s], agrows(c, zz), agrows(c, zz), dev(dz=s)).wait_recv()
            fwd2[c, s] = send(agrows(c, zz, start, 32), agrows(c, zz, start, 32), dev(dz=(s + 2) % 4))[1]

    def gathered(c):
        zz = (z + 2) % 4
        for s, start in ((1, 0), (3, 32)):
            half = agrows(c, zz, start, 32)
            describe(fwd2[c, s], half, half, dev(dz=2)).wait_recv()

    exd, rrd = {}, []

    def token_grad(c):
        gathered(c)
        pg = ag[1, pl.ds(c * 256, 256), :]

        @pl.loop(0, 2)
        def _(n):
            cols = pl.ds(pl.multiple_of(n * 1536, 1536), 1536)
            gt[pl.ds(c * 256, 256), cols] = dot(pg, wi[cols, :], 1, 1).astype(jnp.bfloat16)

        exd[c] = send(gt.at[pl.ds(c * 256 + 128, 128)], ex.at[c], dev(dk=1))[0]
        part = jnp.sum(pg.astype(jnp.float32), axis=0, keepdims=True)
        gbin_ref[...] = part if c == 1 else gbin_ref[...] + part

    def combine(c):
        exd[c].wait_recv()
        own = pl.ds(c * 256, 128)
        gt[own, :] = (gt[own, :].astype(jnp.float32) + ex[c].astype(jnp.float32)).astype(jnp.bfloat16)
        if c == 3:
            rrd.append(send(gt.at[own], rr.at[1], dev(d2=2))[0])
        elif c > 0:
            for i, d2 in enumerate((1, 3)):
                src = gt.at[pl.ds(c * 256 + i * 64, 64)]
                rrd.append(send(src, rr.at[(-d2) % 4 - 1, pl.ds((c - 1) * 64, 64)], dev(d2=d2))[0])

    def end_scatter():
        for cp in rrd:
            cp.wait_recv()
        for i, d1 in enumerate(D1):
            rows = pl.ds(i * 32, 32)
            total = gt[rows, :].astype(jnp.float32)
            for s in range(3):
                total += rr[s, rows, :].astype(jnp.float32)
            if d1 == 0:
                fin[...] = total
            else:
                q2[d1 - 1] = total.astype(jnp.bfloat16)
                r2d.append(send(q2.at[d1 - 1], r2.at[(-d1) % 4 - 1], dev(d1=d1))[0])

    def weight_out_grad(n):
        cols = pl.ds(n * 768, 768)
        wo[:, cols] = dot(ag[0], tc[1, :, cols], 0, 0).astype(jnp.bfloat16)

    def weight_in_grad(n):
        cols = pl.ds(n * 768, 768)
        wi[cols, :] = dot(tc[0, :, cols], ag[1], 0, 0).astype(jnp.bfloat16)

    r2d = []
    first(1)
    first(3)
    spread(0)
    spread(1)
    first(2)
    spread(3)
    spread(2)
    loads[2].wait()
    loads[3].wait()
    loads[4].wait()
    forward(0)
    arrive(0, 1)
    arrive(0, 3)
    pass_on(0)
    arrive(1, 1)
    arrive(1, 3)
    forward(1)
    activate(0)
    arrive(3, 1)
    arrive(3, 3)
    pass_on(1)
    arrive(2, 1)
    arrive(2, 3)
    forward(2)
    activate(1)
    for d1 in D1:
        p2[d1, 2].wait_recv()
        share((d1, 2))
    pass_on(2)
    forward(3)
    relay(1)
    pass_on(3)
    token_grad(1)
    activate(3)
    combine(1)
    activate(2)
    relay(3)
    relay(2)
    token_grad(3)
    relay(0)
    combine(3)
    token_grad(2)
    token_grad(0)
    combine(2)
    combine(0)
    weight_out_grad(0)
    weight_out_grad(1)
    weight_out_grad(2)
    end_scatter()
    weight_out_grad(3)
    for n in range(4):
        weight_in_grad(n)
    for cp in r2d:
        cp.wait_recv()
    total = fin[...]
    for s in range(3):
        total += r2[s].astype(jnp.float32)
    gtok_ref[...] = total.astype(jnp.bfloat16)
    for cp in sent:
        cp.wait_send()


def store(*refs):
    sem = refs[10]
    moves = [pltpu.make_async_copy(refs[i], refs[5 + i], sem.at[i]) for i in (1, 3, 0)]
    moves += [pltpu.make_async_copy(refs[i].at[0], refs[5 + i], sem.at[i]) for i in (2, 4)]
    for cp in moves:
        cp.start()
    for cp in moves:
        cp.wait()


def per_device(tokens, cotangent, weight_in, bias_in, weight_out):
    hbm = pl.BlockSpec(memory_space=pl.ANY)
    bf16, f32 = jnp.bfloat16, jnp.float32
    kept = (((32, 3072), bf16), ((3072, 768), bf16), ((1, 768), f32), ((768, 3072), bf16), ((1, 3072), f32))
    results = pl.pallas_call(
        kernel,
        out_shape=tuple(pltpu.VMEM(shape, dtype) for shape, dtype in kept),
        in_specs=[hbm] * 5,
        out_specs=tuple(pl.BlockSpec(memory_space=pltpu.VMEM) for _ in kept),
        scratch_shapes=[
            pltpu.VMEM((1, 768), f32),
            pltpu.VMEM((2, 1024, 3072), bf16),
            pltpu.VMEM((4, 4, 2, 64, 768), bf16),
            pltpu.VMEM((4, 2, 2, 32, 768), bf16),
            pltpu.VMEM((4, 2, 2, 64, 768), bf16),
            pltpu.VMEM((2, 1024, 768), bf16),
            pltpu.VMEM((1024, 3072), bf16),
            pltpu.VMEM((4, 128, 3072), bf16),
            pltpu.VMEM((3, 128, 3072), bf16),
            pltpu.VMEM((3, 32, 3072), bf16),
            pltpu.VMEM((3, 32, 3072), bf16),
            pltpu.VMEM((32, 3072), f32),
            pltpu.SemaphoreType.DMA((5,)),
            pltpu.SemaphoreType.DMA((N_COPIES,)),
            pltpu.SemaphoreType.DMA((N_COPIES,)),
        ],
        compiler_params=pltpu.CompilerParams(
            collective_id=0, has_side_effects=True, vmem_limit_bytes=46 * 2**20
        ),
        cost_estimate=pl.CostEstimate(flops=24_200_000_000, bytes_accessed=20_000_000, transcendentals=800_000),
    )(tokens, cotangent, weight_in, bias_in, weight_out)
    return pl.pallas_call(
        store,
        out_shape=tuple(
            jax.ShapeDtypeStruct(shape[1:] if shape[0] == 1 else shape, dtype) for shape, dtype in kept
        ),
        in_specs=[pl.BlockSpec(memory_space=pltpu.VMEM)] * 5,
        out_specs=(hbm,) * 5,
        scratch_shapes=[pltpu.SemaphoreType.DMA((5,))],
        compiler_params=pltpu.CompilerParams(vmem_limit_bytes=2**20),
    )(*results)


def solution(mesh):
    placed = (P("col", "row"), P("col", "row"), P("row", "col"), P("col"), P("col", "row"))
    return jax.shard_map(
        per_device,
        mesh=mesh,
        in_specs=placed,
        out_specs=(P("col", "row"), P("row", "col"), P("col"), P("col", "row"), P("row")),
        check_vma=False,
    )
```

time: 133 us -> 114 us (0.86)
  local copies, waits for them, and re-layouts: 10.7 us -> 0 us
  Pallas kernels: 120 us -> 113 us
    unnamed x10 -> x0, local copies, waits for them, and re-layouts: 9.45 us -> none
    pallas_call x1 -> x2, Pallas kernels: 120 us -> 113 us  [the longest x1 109 us: per_device(): pl.pallas_call(kernel, out_shape=tuple((pltpu.VMEM(shape, dtype) for shap...]
where the time goes in v2:
time: 114 us
  Pallas kernels  113 us (99%)
    pallas_call x1, Pallas kernels, per_device(): pl.pallas_call(kernel, out_shape=tuple((pltpu.VMEM(shape, dtype) for shap...  109 us
    pallas_call x1, Pallas kernels, per_device(): pl.pallas_call(store, out_shape=tuple((jax.ShapeDtypeStruct(shape[1:] if...  3.79 us

profile of v2, /device:TPU:1, one launch (start us, length us, event | category | flops | bytes accessed | tf_op | source)
XLA Modules:
  0.0 113.6 jit_solution(7327779850365687721)
XLA Ops:
  0.6 109.0 %shard_map.92 = (bf16[32,3072]{1,0:T(8,128)(2,1)S(1)}, bf16[3072,768]{1,0:T(8,128)(2,1)S(1)}, f32[1,768]{1,0:T(1,128)S(1)}, bf16[768,3072]{1,0:T(8,128)(2,1)S(1)}, f32[1,3072]{1,0:T(1,128)S(1)}) custom-call(bf16[32,3072]{1,0:T(8,128)(2,1)} %tok_hbm.1, bf16[32,3072]{1,0:T(8,128)(2,1)} %cot_hbm.1, bf16[3072,768]{1,0:T(8,128)(2,1)} %win_hbm.1, f32[768]{0:T(1024)} %bias_hbm.1, ...), custom_call_target="tpu_custom_call" | custom-call | flops 24199999488 | bytes 20000000 | tf_op jit(solution)/shard_map/pallas_call | solution.py:296
  109.7 3.8 %shard_map.93 = (bf16[32,3072]{1,0:T(8,128)(2,1)}, bf16[3072,768]{1,0:T(8,128)(2,1)}, f32[768]{0:T(1024)}, bf16[768,3072]{1,0:T(8,128)(2,1)}, f32[3072]{0:T(1024)}) custom-call(bf16[32,3072]{1,0:T(8,128)(2,1)S(1)} %get-tuple-element.10.refs_0_, bf16[3072,768]{1,0:T(8,128)(2,1)S(1)} %get-tuple-element.11.refs_1_, f32[1,768]{1,0:T(1,128)S(1)} %get-tuple-element.12.refs_2_, ...), custom_call_target="tpu_custom_call" | custom-call | tf_op jit(solution)/shard_map/pallas_call | solution.py:323

commit v3 on v2

v3 whole, which is shorter than its diff:
```python
import jax
import jax.numpy as jnp
from jax import lax
from jax.experimental import pallas as pl
from jax.experimental.pallas import tpu as pltpu
from jax.sharding import PartitionSpec as P

MESH = pl.DeviceIdType.MESH
coeff = 0.7978845608
N_COPIES = 160
D1 = (0, 1, 3, 2)
CHUNKS = (
    ((0, 0), (1, 0), (3, 0)),
    ((2, 0), (0, 1), (0, 3)),
    ((1, 1), (1, 3), (3, 1), (3, 3)),
    ((0, 2), (1, 2), (2, 1), (2, 3)),
    ((3, 2), (2, 2)),
)
SIZE = [64 * len(blocks) for blocks in CHUNKS]
ORDER = (0, 1, 4, 2, 3)
BASE = {c: sum(SIZE[d] for d in ORDER[:i]) for i, c in enumerate(ORDER)}
ROW = {b: BASE[c] + i * 32 for c, blocks in enumerate(CHUNKS) for i, b in enumerate(blocks)}
HALF = {b: SIZE[c] // 2 for c, blocks in enumerate(CHUNKS) for b in blocks}


def act_parts(preact, hidden_grad):
    cube = preact * preact * preact
    tangent = jnp.tanh(coeff * (preact + 0.044715 * cube))
    activated = (0.5 * preact * (1.0 + tangent)).astype(jnp.bfloat16)
    slope = 0.5 * (1.0 + tangent) + 0.5 * preact * (1.0 - tangent * tangent) * coeff * (
        1.0 + 0.134145 * preact * preact
    )
    return (activated, (hidden_grad * slope).astype(jnp.bfloat16))


def dot(a, b, ca, cb):
    return lax.dot_general(a, b, (((ca,), (cb,)), ((), ())), preferred_element_type=jnp.float32)


def kernel(
    tok_hbm, cot_hbm, win_hbm, bias_hbm, wout_hbm,
    gtok_ref, wi, gbin_ref, wo, gbout_ref,
    bias, tc, pb, za, zr, ag, gt, ex, rr, q2, r2, fin, acc, lsem, ssem, rsem,
):
    z = lax.axis_index("row")
    col = lax.axis_index("col")
    y, x, k = col // 8, (col // 2) % 4, col % 2

    def dev(d1=0, d2=0, dz=0, dk=0, turn=0):
        dx, dy = (d2, d1) if turn else (d1, d2)
        return ((z + dz) % 4, ((y + dy) % 4) * 8 + ((x + dx) % 4) * 2 + (k + dk) % 2)

    used = [0]
    sent = []

    def describe(i, src, dst, device):
        return pltpu.make_async_remote_copy(
            src_ref=src, dst_ref=dst, send_sem=ssem.at[i], recv_sem=rsem.at[i], device_id=device, device_id_type=MESH
        )

    def send(src, dst, device):
        i = used[0]
        used[0] += 1
        cp = describe(i, src, dst, device)
        cp.start()
        sent.append(cp)
        return cp, i

    loads = [
        pltpu.make_async_copy(tok_hbm, tc.at[0, pl.ds(0, 32)], lsem.at[0]),
        pltpu.make_async_copy(cot_hbm, tc.at[1, pl.ds(0, 32)], lsem.at[1]),
        pltpu.make_async_copy(win_hbm, wi, lsem.at[2]),
        pltpu.make_async_copy(wout_hbm, wo, lsem.at[3]),
        pltpu.make_async_copy(bias_hbm, bias.at[0], lsem.at[4]),
    ]
    for cp in loads:
        cp.start()

    barrier = pltpu.get_barrier_semaphore()
    greeted = [dev(dk=1)]
    for o in (1, 2, 3):
        greeted += [dev(d1=o), dev(d2=o), dev(dz=o)]
    for device in greeted:
        pl.semaphore_signal(barrier, inc=1, device_id=device, device_id_type=MESH)
    pl.semaphore_wait(barrier, len(greeted))

    def block(row):
        return tc.at[:, pl.ds(row, 32)]

    p1, p2, sib = {}, {}, {}

    def share(b):
        sib[b] = send(block(ROW[b]), block(ROW[b] + HALF[b]), dev(dk=1))[0]

    def piece(row, turn):
        return tc.at[:, pl.ds(row + 16 * turn, 16)]

    def to_first(o):
        row = ROW[(-o) % 4, 0]
        p1[(-o) % 4] = [
            send(own.at[pl.ds(16 * t, 16)], tc.at[i, pl.ds(row + 16 * t, 16)], dev(d1=o, turn=t))[0]
            for i, own in enumerate((tok_hbm, cot_hbm))
            for t in (0, 1)
        ]

    def to_far():
        p1[2] = []
        for i, (d1, o) in enumerate(((1, 3), (3, 1))):
            for t in (0, 1):
                src, dst = (tc.at[i, pl.ds(ROW[d, 0] + 16 * t, 16)] for d in (d1, 2))
                p1[2].append(send(src, dst, dev(d1=o, turn=t))[0])

    def first(d1):
        for cp in p1[d1]:
            cp.wait_recv()
        share((d1, 0))

    def to_second(src, dst, o):
        return [send(piece(ROW[src], t), piece(ROW[dst], t), dev(d2=o, turn=t))[0] for t in (0, 1)]

    def spread(d1):
        for o in (1, 3):
            d2 = (-o) % 4
            p2[d1, d2] = to_second((d1, 0), (d1, d2), o)

    def receive(d1, d2):
        for cp in p2[d1, d2]:
            cp.wait_recv()
        share((d1, d2))

    def arrive(d1, d2):
        receive(d1, d2)
        if (d2 == 1 and d1 in (0, 3)) or (d2 == 3 and d1 in (1, 2)):
            p2[d1, 2] = to_second((d1, d2), (d1, 2), (d2 + 2) % 4)

    zs, agd, fwd2 = {}, {}, {}

    def quarter(c, zz):
        n = SIZE[c] // 4
        return pl.ds(pl.multiple_of(BASE[c] + (zz % 4) * n, n), n)

    def slot(c):
        return pl.ds(BASE[c] // 4, SIZE[c] // 4)

    def forward(c):
        for b in CHUNKS[c]:
            sib[b].wait_recv()
        rows = pl.ds(BASE[c], SIZE[c])
        for i, w in enumerate((wi, wo)):
            pb[i, rows, :] = dot(tc[i, rows, :], w[...], 1, i).astype(jnp.bfloat16)
            near, far = (3, 1) if i == 0 else (1, 3)
            zs[c, i, "far"] = send(pb.at[i, quarter(c, z + 2)], za.at[i, slot(c)], dev(dz=far))[0]
            zs[c, 1 - i, "near"] = send(pb.at[i, quarter(c, z + near)], zr.at[1 - i, i, slot(c)], dev(dz=near))[0]

    def bias_out(c):
        cot = tc[1, pl.ds(BASE[c], SIZE[c]), :]
        total = jnp.sum(cot.astype(jnp.float32), axis=0, keepdims=True)
        gbout_ref[...] = total if c == 0 else gbout_ref[...] + total

    def pass_on(c):
        for i, o in enumerate((1, 3)):
            zs[c, i, "far"].wait_recv()
            there = quarter(c, z + o)
            both = pb[i, there, :].astype(jnp.float32) + za[i, slot(c), :].astype(jnp.float32)
            pb[i, there, :] = both.astype(jnp.bfloat16)
            zs[c, i, "sum"] = send(pb.at[i, there], zr.at[i, i, slot(c)], dev(dz=o))[0]

    def activate(c):
        for i in range(2):
            zs[c, i, "near"].wait_recv()
            zs[c, i, "sum"].wait_recv()
        mine = quarter(c, z)
        u = bias[...] + pb[0, mine, :].astype(jnp.float32)
        h = pb[1, mine, :].astype(jnp.float32)
        for i in range(2):
            u += zr[i, 0, slot(c), :].astype(jnp.float32)
            h += zr[i, 1, slot(c), :].astype(jnp.float32)
        activated, preact_grad = act_parts(u, h)
        ag[0, mine, :] = activated
        ag[1, mine, :] = preact_grad
        for o in (1, 3):
            agd[c, (-o) % 4] = send(ag.at[:, mine], ag.at[:, mine], dev(dz=o))[1]

    def relay(c):
        for i, s in enumerate((1, 3)):
            there = quarter(c, z + s)
            describe(agd[c, s], ag.at[:, there], ag.at[:, there], dev(dz=s)).wait_recv()
            fwd2[c, i] = send(ag.at[i, there], ag.at[i, there], dev(dz=(s + 2) % 4))[1]

    def gathered(c):
        for i in range(2):
            there = ag.at[i, quarter(c, z + 2)]
            describe(fwd2[c, i], there, there, dev(dz=2)).wait_recv()

    exd, rrd = {}, {}

    def token_grad(c):
        gathered(c)
        rows = pl.ds(BASE[c], SIZE[c])
        pg = ag[1, rows, :]

        @pl.loop(0, 2)
        def _(n):
            cols = pl.ds(pl.multiple_of(n * 1536, 1536), 1536)
            gt[rows, cols] = dot(pg, wi[cols, :], 1, 1).astype(jnp.bfloat16)

        h = SIZE[c] // 2
        exd[c] = send(gt.at[pl.ds(BASE[c] + h, h)], ex.at[pl.ds(BASE[c] // 2, h)], dev(dk=1))[0]
        total = jnp.sum(pg.astype(jnp.float32), axis=0, keepdims=True)
        gbin_ref[...] = total if c == 2 else gbin_ref[...] + total

    def combine(c):
        exd[c].wait_recv()
        h = SIZE[c] // 2
        own = pl.ds(BASE[c], h)
        other = ex[pl.ds(BASE[c] // 2, h), :].astype(jnp.float32)
        gt[own, :] = (gt[own, :].astype(jnp.float32) + other).astype(jnp.bfloat16)
        for d1, d2 in CHUNKS[c]:
            if d2:
                rrd[d1, d2] = []
                for t in (0, 1):
                    src = gt.at[pl.ds(ROW[d1, d2] + 16 * t, 16)]
                    dst = rr.at[(-d2) % 4 - 1, pl.ds(D1.index(d1) * 32 + 16 * t, 16)]
                    rrd[d1, d2].append(send(src, dst, dev(d2=d2, turn=t))[0])

    def end_scatter(d1):
        total = gt[pl.ds(ROW[d1, 0], 32), :].astype(jnp.float32)
        for d2 in (1, 3, 2):
            for cp in rrd[d1, d2]:
                cp.wait_recv()
            total += rr[(-d2) % 4 - 1, pl.ds(D1.index(d1) * 32, 32), :].astype(jnp.float32)
        if d1 == 0:
            fin[...] = total
        else:
            q2[d1 - 1] = total.astype(jnp.bfloat16)
            for t in (0, 1):
                rows = pl.ds(16 * t, 16)
                r2d.append(send(q2.at[d1 - 1, rows], r2.at[(-d1) % 4 - 1, rows], dev(d1=d1, turn=t))[0])

    def weight_out_part(n):
        cols, late = pl.ds(n * 768, 768), pl.ds(512, 512)
        acc[:, cols] = dot(ag[0, late, :], tc[1, late, cols], 0, 0)

    def weight_out_grad(n):
        cols, early = pl.ds(n * 768, 768), pl.ds(0, 512)
        total = acc[:, cols] + dot(ag[0, early, :], tc[1, early, cols], 0, 0)
        wo[:, cols] = total.astype(jnp.bfloat16)

    def weight_in_grad(n):
        cols = pl.ds(n * 768, 768)
        wi[cols, :] = dot(tc[0, :, cols], ag[1], 0, 0).astype(jnp.bfloat16)

    r2d = []
    to_first(1)
    to_first(3)
    loads[0].wait()
    loads[1].wait()
    share((0, 0))
    first(1)
    first(3)
    to_far()
    spread(0)
    spread(1)
    spread(3)
    loads[2].wait()
    loads[3].wait()
    loads[4].wait()
    forward(0)
    first(2)
    spread(2)
    arrive(0, 1)
    arrive(0, 3)
    pass_on(0)
    forward(1)
    activate(0)
    bias_out(0)
    arrive(1, 1)
    arrive(1, 3)
    pass_on(1)
    arrive(3, 1)
    arrive(3, 3)
    forward(2)
    activate(1)
    bias_out(1)
    receive(0, 2)
    receive(1, 2)
    pass_on(2)
    arrive(2, 1)
    arrive(2, 3)
    forward(3)
    activate(2)
    bias_out(2)
    receive(3, 2)
    receive(2, 2)
    pass_on(3)
    relay(2)
    forward(4)
    activate(3)
    pass_on(4)
    bias_out(3)
    token_grad(2)
    relay(3)
    activate(4)
    combine(2)
    relay(1)
    token_grad(3)
    relay(4)
    weight_out_part(0)
    combine(3)
    relay(0)
    weight_out_part(1)
    token_grad(4)
    weight_out_part(2)
    combine(4)
    token_grad(1)
    weight_out_part(3)
    token_grad(0)
    combine(1)
    bias_out(4)
    combine(0)
    end_scatter(1)
    end_scatter(0)
    weight_out_grad(0)
    end_scatter(2)
    end_scatter(3)
    weight_out_grad(1)
    weight_out_grad(2)
    weight_out_grad(3)
    for n in range(4):
        weight_in_grad(n)
    for cp in r2d:
        cp.wait_recv()
    total = fin[...]
    for s in range(3):
        total += r2[s].astype(jnp.float32)
    gtok_ref[...] = total.astype(jnp.bfloat16)
    for cp in sent:
        cp.wait_send()


def store(*refs):
    sem = refs[10]
    moves = [pltpu.make_async_copy(refs[i], refs[5 + i], sem.at[i]) for i in (1, 3, 0)]
    moves += [pltpu.make_async_copy(refs[i].at[0], refs[5 + i], sem.at[i]) for i in (2, 4)]
    for cp in moves:
        cp.start()
    for cp in moves:
        cp.wait()


def per_device(tokens, cotangent, weight_in, bias_in, weight_out):
    hbm = pl.BlockSpec(memory_space=pl.ANY)
    bf16, f32 = jnp.bfloat16, jnp.float32
    kept = (((32, 3072), bf16), ((3072, 768), bf16), ((1, 768), f32), ((768, 3072), bf16), ((1, 3072), f32))
    results = pl.pallas_call(
        kernel,
        out_shape=tuple(pltpu.VMEM(shape, dtype) for shape, dtype in kept),
        in_specs=[hbm] * 5,
        out_specs=tuple(pl.BlockSpec(memory_space=pltpu.VMEM) for _ in kept),
        scratch_shapes=[
            pltpu.VMEM((1, 768), f32),
            pltpu.VMEM((2, 1024, 3072), bf16),
            pltpu.VMEM((2, 1024, 768), bf16),
            pltpu.VMEM((2, 256, 768), bf16),
            pltpu.VMEM((2, 2, 256, 768), bf16),
            pltpu.VMEM((2, 1024, 768), bf16),
            pltpu.VMEM((1024, 3072), bf16),
            pltpu.VMEM((512, 3072), bf16),
            pltpu.VMEM((3, 128, 3072), bf16),
            pltpu.VMEM((3, 32, 3072), bf16),
            pltpu.VMEM((3, 32, 3072), bf16),
            pltpu.VMEM((32, 3072), f32),
            pltpu.VMEM((768, 3072), f32),
            pltpu.SemaphoreType.DMA((5,)),
            pltpu.SemaphoreType.DMA((N_COPIES,)),
            pltpu.SemaphoreType.DMA((N_COPIES,)),
        ],
        compiler_params=pltpu.CompilerParams(
            collective_id=0, has_side_effects=True, vmem_limit_bytes=50 * 2**20
        ),
        cost_estimate=pl.CostEstimate(flops=24_200_000_000, bytes_accessed=20_000_000, transcendentals=800_000),
    )(tokens, cotangent, weight_in, bias_in, weight_out)
    return pl.pallas_call(
        store,
        out_shape=tuple(
            jax.ShapeDtypeStruct(shape[1:] if shape[0] == 1 else shape, dtype) for shape, dtype in kept
        ),
        in_specs=[pl.BlockSpec(memory_space=pltpu.VMEM)] * 5,
        out_specs=(hbm,) * 5,
        scratch_shapes=[pltpu.SemaphoreType.DMA((5,))],
        compiler_params=pltpu.CompilerParams(vmem_limit_bytes=2**20),
    )(*results)


def solution(mesh):
    placed = (P("col", "row"), P("col", "row"), P("row", "col"), P("col"), P("col", "row"))
    return jax.shard_map(
        per_device,
        mesh=mesh,
        in_specs=placed,
        out_specs=(P("col", "row"), P("row", "col"), P("col"), P("col", "row"), P("row")),
        check_vma=False,
    )
```

time: 114 us -> 108 us (0.947)
  Pallas kernels: 113 us -> 107 us
    pallas_call x1, Pallas kernels: 109 us -> 104 us  [per_device(): pl.pallas_call(kernel, out_shape=tuple((pltpu.VMEM(shape, dtype) for shap...]
where the time goes in v3:
time: 108 us
  Pallas kernels  107 us (99%)
    pallas_call x1, Pallas kernels, per_device(): pl.pallas_call(kernel, out_shape=tuple((pltpu.VMEM(shape, dtype) for shap...  104 us
    pallas_call x1, Pallas kernels, per_device(): pl.pallas_call(store, out_shape=tuple((jax.ShapeDtypeStruct(shape[1:] if...  3.79 us

profile of v3, /device:TPU:1, one launch (start us, length us, event | category | flops | bytes accessed | tf_op | source)
XLA Modules:
  0.0 108.2 jit_solution(3868104906878530613)
XLA Ops:
  0.6 103.6 %shard_map.92 = (bf16[32,3072]{1,0:T(8,128)(2,1)S(1)}, bf16[3072,768]{1,0:T(8,128)(2,1)S(1)}, f32[1,768]{1,0:T(1,128)S(1)}, bf16[768,3072]{1,0:T(8,128)(2,1)S(1)}, f32[1,3072]{1,0:T(1,128)S(1)}) custom-call(bf16[32,3072]{1,0:T(8,128)(2,1)} %tok_hbm.1, bf16[32,3072]{1,0:T(8,128)(2,1)} %cot_hbm.1, bf16[3072,768]{1,0:T(8,128)(2,1)} %win_hbm.1, f32[768]{0:T(1024)} %bias_hbm.1, ...), custom_call_target="tpu_custom_call" | custom-call | flops 24199999488 | bytes 20000000 | tf_op jit(solution)/shard_map/pallas_call | solution.py:355
  104.2 3.8 %shard_map.93 = (bf16[32,3072]{1,0:T(8,128)(2,1)}, bf16[3072,768]{1,0:T(8,128)(2,1)}, f32[768]{0:T(1024)}, bf16[768,3072]{1,0:T(8,128)(2,1)}, f32[3072]{0:T(1024)}) custom-call(bf16[32,3072]{1,0:T(8,128)(2,1)S(1)} %get-tuple-element.10.refs_0_, bf16[3072,768]{1,0:T(8,128)(2,1)S(1)} %get-tuple-element.11.refs_1_, f32[1,768]{1,0:T(1,128)S(1)} %get-tuple-element.12.refs_2_, ...), custom_call_target="tpu_custom_call" | custom-call | tf_op jit(solution)/shard_map/pallas_call | solution.py:383

commit v4 on v3

--- a/solution.py
+++ b/solution.py
@@ -12,8 +12,8 @@
 CHUNKS = (
     ((0, 0), (1, 0), (3, 0)),
     ((2, 0), (0, 1), (0, 3)),
-    ((1, 1), (1, 3), (3, 1), (3, 3)),
-    ((0, 2), (1, 2), (2, 1), (2, 3)),
+    ((1, 1), (1, 3), (2, 1), (2, 3)),
+    ((0, 2), (1, 2), (3, 1), (3, 3)),
     ((3, 2), (2, 2)),
 )
 SIZE = [64 * len(blocks) for blocks in CHUNKS]
@@ -260,36 +260,33 @@
     first(3)
     to_far()
     spread(0)
-    spread(1)
-    spread(3)
     loads[2].wait()
     loads[3].wait()
     loads[4].wait()
     forward(0)
+    spread(1)
     first(2)
     spread(2)
+    spread(3)
     arrive(0, 1)
     arrive(0, 3)
     pass_on(0)
     forward(1)
-    activate(0)
-    bias_out(0)
     arrive(1, 1)
     arrive(1, 3)
+    activate(0)
     pass_on(1)
+    arrive(2, 1)
+    arrive(2, 3)
+    forward(2)
     arrive(3, 1)
     arrive(3, 3)
-    forward(2)
     activate(1)
-    bias_out(1)
+    pass_on(2)
     receive(0, 2)
     receive(1, 2)
-    pass_on(2)
-    arrive(2, 1)
-    arrive(2, 3)
     forward(3)
     activate(2)
-    bias_out(2)
     receive(3, 2)
     receive(2, 2)
     pass_on(3)
@@ -297,26 +294,29 @@
     forward(4)
     activate(3)
     pass_on(4)
-    bias_out(3)
+    bias_out(0)
     token_grad(2)
     relay(3)
     activate(4)
     combine(2)
     relay(1)
+    bias_out(1)
     token_grad(3)
     relay(4)
     weight_out_part(0)
     combine(3)
     relay(0)
     weight_out_part(1)
+    bias_out(2)
     token_grad(4)
     weight_out_part(2)
     combine(4)
+    bias_out(3)
     token_grad(1)
     weight_out_part(3)
+    bias_out(4)
     token_grad(0)
     combine(1)
-    bias_out(4)
     combine(0)
     end_scatter(1)
     end_scatter(0)

time: 108 us -> 107 us (level)
    pallas_call x1, Pallas kernels: 104 us -> 102 us  [per_device(): pl.pallas_call(kernel, out_shape=tuple((pltpu.VMEM(shape, dtype) for shap...]
where the time goes in v4:
time: 107 us; the launch traced here: 106 us
  Pallas kernels  106 us (99%)
    pallas_call x1, Pallas kernels, per_device(): pl.pallas_call(kernel, out_shape=tuple((pltpu.VMEM(shape, dtype) for shap...  102 us
    pallas_call x1, Pallas kernels, per_device(): pl.pallas_call(store, out_shape=tuple((jax.ShapeDtypeStruct(shape[1:] if...  3.79 us

profile of v4, /device:TPU:1, one launch (start us, length us, event | category | flops | bytes accessed | tf_op | source)
XLA Modules:
  0.0 106.5 jit_solution(945321759464693726)
XLA Ops:
  0.6 101.8 %shard_map.92 = (bf16[32,3072]{1,0:T(8,128)(2,1)S(1)}, bf16[3072,768]{1,0:T(8,128)(2,1)S(1)}, f32[1,768]{1,0:T(1,128)S(1)}, bf16[768,3072]{1,0:T(8,128)(2,1)S(1)}, f32[1,3072]{1,0:T(1,128)S(1)}) custom-call(bf16[32,3072]{1,0:T(8,128)(2,1)} %tok_hbm.1, bf16[32,3072]{1,0:T(8,128)(2,1)} %cot_hbm.1, bf16[3072,768]{1,0:T(8,128)(2,1)} %win_hbm.1, f32[768]{0:T(1024)} %bias_hbm.1, ...), custom_call_target="tpu_custom_call" | custom-call | flops 24199999488 | bytes 20000000 | tf_op jit(solution)/shard_map/pallas_call | solution.py:355
  102.5 3.8 %shard_map.93 = (bf16[32,3072]{1,0:T(8,128)(2,1)}, bf16[3072,768]{1,0:T(8,128)(2,1)}, f32[768]{0:T(1024)}, bf16[768,3072]{1,0:T(8,128)(2,1)}, f32[3072]{0:T(1024)}) custom-call(bf16[32,3072]{1,0:T(8,128)(2,1)S(1)} %get-tuple-element.10.refs_0_, bf16[3072,768]{1,0:T(8,128)(2,1)S(1)} %get-tuple-element.11.refs_1_, f32[1,768]{1,0:T(1,128)S(1)} %get-tuple-element.12.refs_2_, ...), custom_call_target="tpu_custom_call" | custom-call | tf_op jit(solution)/shard_map/pallas_call | solution.py:383
